TPU v7x, 512 devices: a whole 4x4x16 slice. The times are simulated.
512 devices in a mesh: seq: 32 (over z, core), chan: 16 (over y, x).
Axes of the slice: x: 4, y: 4, z: 16, core: 2. Of those that a mesh axis runs over, the one named last changes fastest.
Arguments:
- arrived: bfloat16 [3, 16384, 8192], P(None, ('seq', 'chan')), may hold values from -6 to 6
- landing: int32 [32, 32], P('seq'), may hold values from 0 to 31, each once within a row
- resets: int32 [16384], P('seq'), may hold values 0 or 1
- short_taps: float32 [3, 7, 8192], P(None, None, 'chan'), may hold values from -3 to 3
- decay_rate: float32 [16, 8192], P(None, 'chan'), may hold values from 0 to 1, as said below
- residues: float32 [16, 8192], P(None, 'chan'), may hold values from -2 to 2
- skip_gain: float32 [8192], P('chan'), may hold values from 0.5 to 1.5
Outputs:
- mixed: bfloat16 [16384, 8192], P('seq', 'chan')
Inputs may be any that keep to these rules, and one draw needn't show every extreme that they name: Each row is a permutation: landing[r, s] is the place, among the blocks of shard r, of the block that comes from loader group s. `resets`: 1 marks the first token of a document. `decay_rate`: positive decay rates.
All inputs are finite; a program needn't handle non-finite values. No bound on the sum of `resets` on one device may be relied on, other than what follows from the above.
Results may differ from a plain program's by a relative error of at most 0.01.
Values may be sent and summed in bfloat16 or wider, within the bound.
A program may use at most 64 MiB of HBM per device.

v0:
```python
import jax
import jax.numpy as jnp
from jax import lax
from jax.sharding import PartitionSpec as P


def passed_along(shard, axis, by):
    count = lax.axis_size(axis)
    pairs = [(i, i + by) for i in range(count) if 0 <= i + by < count]
    return lax.ppermute(shard, axis, pairs)


def short_filter(extended, tap_table, out_rows):
    tap_count = tap_table.shape[1]
    combined = jnp.zeros((extended.shape[0], out_rows, extended.shape[2]), jnp.float32)
    for tap_index in range(tap_count):
        offset_rows = tap_count - 1 - tap_index
        combined = (
            combined
            + tap_table[:, tap_index][:, None, :]
            * extended[:, offset_rows : offset_rows + out_rows, :]
        )
    return combined


def modal_local(gated_mix, resets, decay_rates, mode_gain):
    length, channels = gated_mix.shape
    modes = decay_rates.shape[0]
    block_len = 64
    blocks = length // block_len
    offsets = jnp.arange(block_len, dtype=jnp.float32)
    growth = jnp.exp(offsets[:, None, None] * decay_rates[None])
    shrink = jnp.exp(-offsets[:, None, None] * decay_rates[None])
    decay_step = jnp.exp(-decay_rates)
    doc_ids = jnp.cumsum(resets)
    row_ids = lax.broadcasted_iota(jnp.int32, (block_len, block_len), 0)
    col_ids = lax.broadcasted_iota(jnp.int32, (block_len, block_len), 1)

    def advance(carried_state, inputs):
        values, block_docs, reset_marks = inputs
        same_doc = ((block_docs[:, None] == block_docs[None, :]) & (col_ids <= row_ids)).astype(
            jnp.float32
        )
        lifted = (growth * values.astype(jnp.float32)[:, None, :]).reshape(
            block_len, modes * channels
        )
        summed = jnp.dot(same_doc, lifted, precision=lax.Precision.HIGHEST).reshape(
            block_len, modes, channels
        )
        untouched = (jnp.cumsum(reset_marks) == 0).astype(jnp.float32)
        inner_sum = summed + untouched[:, None, None] * (decay_step * carried_state)[None]
        states = shrink * inner_sum
        return (states[-1], jnp.sum(mode_gain[None] * states, axis=1))

    end_state, outputs = lax.scan(
        advance,
        jnp.zeros((modes, channels), jnp.float32),
        (
            gated_mix.reshape(blocks, block_len, channels),
            doc_ids.reshape(blocks, block_len),
            resets.reshape(blocks, block_len),
        ),
    )
    return (end_state, outputs.reshape(length, channels))


def modal_carry(entering, resets, decay_rates, mode_gain):
    length = resets.shape[0]
    channels = entering.shape[1]
    block_len = 64
    blocks = length // block_len
    untouched = (jnp.cumsum(resets) == 0).astype(jnp.float32).reshape(blocks, block_len)
    places = (jnp.arange(length, dtype=jnp.float32) + 1.0).reshape(blocks, block_len)
    weighted = mode_gain * entering

    def one_block(inputs):
        powers, keep_mask = inputs
        factor = jnp.exp(-powers[:, None, None] * decay_rates[None])
        return keep_mask[:, None] * jnp.sum(weighted[None] * factor, axis=1)

    result = lax.map(one_block, (places, untouched))
    return result.reshape(length, channels)


def on_device(arrived, landing, resets, short_taps, decay_rate, residues, skip_gain):
    shards = lax.axis_size("seq")
    regrouped = lax.all_to_all(
        lax.all_to_all(arrived, "chan", split_axis=2, concat_axis=1, tiled=True),
        "seq",
        split_axis=1,
        concat_axis=1,
        tiled=True,
    )
    kinds, length, channels = regrouped.shape
    slab_rows = length // shards
    slot_ids = lax.broadcasted_iota(jnp.int32, (shards, shards), 0)
    group_ids = lax.broadcasted_iota(jnp.int32, (shards, shards), 1)
    matches = (landing[0][None, :] == slot_ids).astype(jnp.int32)
    source = jnp.sum(matches * group_ids, axis=1)
    ordered = jnp.take(
        regrouped.reshape(kinds, shards, slab_rows, channels), source, axis=1
    ).reshape(kinds, length, channels)
    short_reach = short_taps.shape[1]
    border = passed_along(ordered[:, length - (short_reach - 1) :, :], "seq", 1)
    filtered = short_filter(jnp.concatenate([border, ordered], axis=1), short_taps, length)
    front_conv = filtered[0]
    gated_mix = (filtered[1] * filtered[2]).astype(jnp.bfloat16)
    mode_gain = residues * jnp.sqrt(-jnp.expm1(-2.0 * decay_rate))
    end_state, local_part = modal_local(gated_mix, resets, decay_rate, mode_gain)
    through = jnp.exp(-decay_rate * length) * (jnp.sum(resets) == 0).astype(jnp.float32)
    all_through, all_end = (
        lax.all_gather(through[None], "seq", axis=0, tiled=True),
        lax.all_gather(end_state[None], "seq", axis=0, tiled=True),
    )
    position = lax.axis_index("seq")

    def absorb(shard_idx, carried_state):
        updated = all_through[shard_idx] * carried_state + all_end[shard_idx]
        return jnp.where(shard_idx < position, updated, carried_state)

    entering = lax.fori_loop(0, all_end.shape[0], absorb, jnp.zeros_like(end_state))
    carried = modal_carry(entering, resets, decay_rate, mode_gain)
    combined = local_part + carried + skip_gain[None, :] * gated_mix.astype(jnp.float32)
    return (front_conv * combined).astype(jnp.bfloat16)


def solution(mesh):
    in_specs = (
        P(None, ("seq", "chan"), None),
        P("seq", None),
        P("seq"),
        P(None, None, "chan"),
        P(None, "chan"),
        P(None, "chan"),
        P("chan"),
    )
    out_specs = P("seq", "chan")
    return jax.shard_map(
        on_device, mesh=mesh, in_specs=in_specs, out_specs=out_specs, check_vma=False
    )
```

profile of v0, /device:TPU:1, one launch (start us, length us, event | category | flops | bytes accessed | tf_op | source)
XLA Modules:
  0.0 374.7 jit_solution(4056098198263031884)
XLA Ops:
  6.5 10.6 %copy.25 = bf16[3,32,8192]{1,0,2:T(4,128)(2,1)} copy(bf16[3,32,8192]{2,1,0:T(8,128)(2,1)} %param.13) | data formatting | bytes 3145728 | tf_op args[0]
  17.2 12.1 %reshape.204 = bf16[16,2,24576]{2,1,0:T(2,128)(2,1)S(1)} reshape(bf16[8192,3,32]{2,1,0:T(4,128)(2,1)} %bitcast.122) | data formatting | bytes 3145728
  29.3 28.7 %all_to_all.23 = bf16[16,2,24576]{2,1,0:T(2,128)(2,1)S(1)} all-to-all(bf16[16,2,24576]{2,1,0:T(2,128)(2,1)S(1)} %reshape.204), channel_id=1, replica_groups=mesh['seq'=32,'chan'=16] {'chan'}, dimensions={0} | all-to-all | bytes 3145728 | tf_op jit(solution)/shard_map/all_to_all | solution.py:88
  58.0 9.4 %reshape.205 = bf16[8192,3,32]{2,1,0:T(4,128)(2,1)} reshape(bf16[16,2,24576]{2,1,0:T(2,128)(2,1)S(1)} %all_to_all.23) | data formatting | bytes 3145728
  67.3 10.5 %copy.32 = bf16[3,32,16,512]{3,1,2,0:T(8,128)(2,1)S(1)} copy(bf16[3,32,16,512]{1,0,3,2:T(4,128)(2,1)} %bitcast.121) | data formatting | bytes 3145728 | tf_op jit(solution)/shard_map/all_to_all | solution.py:88
  77.8 2.7 copy.28
  80.6 17.8 %all-to-all-start.1 = ((bf16[3,512,512]{2,0,1:T(4,128)(2,1)}), bf16[3,512,512]{2,0,1:T(4,128)(2,1)S(1)}, u32[]{:S(2)}, u32[]{:S(2)}) async-start(bf16[3,512,512]{2,0,1:T(4,128)(2,1)} %copy.28), calls=%async_computation.1 | async-start | bytes 4194304 | tf_op jit(solution)/shard_map/all_to_all | solution.py:87
  101.7 100.7 %all-to-all-done.1 = bf16[3,512,512]{2,0,1:T(4,128)(2,1)S(1)} async-done(((bf16[3,512,512]{2,0,1:T(4,128)(2,1)}), bf16[3,512,512]{2,0,1:T(4,128)(2,1)S(1)}, u32[]{:S(2)}, u32[]{:S(2)}) %all-to-all-start.1) | async-done | bytes 1572896 | tf_op jit(solution)/shard_map/all_to_all | solution.py:87
  203.9 2.1 gather_fusion
  207.6 4.7 %collective-permute-start = (bf16[3,6,512]{2,1,0:T(8,128)(2,1)S(1)}, bf16[3,6,512]{2,1,0:T(8,128)(2,1)S(1)}, u32[]{:S(2)}, u32[]{:S(2)}) collective-permute-start(bf16[3,6,512]{2,1,0:T(8,128)(2,1)S(1)} %slice.87), channel_id=1, source_target_pairs={{0,16},{16,32},{32,48},{48,64},{64,80},{80,96},{96,112},{112,128},... | collective-permute-start | bytes 55304 | tf_op jit(solution)/shard_map/ppermute | solution.py:10
  213.1 6.9 %multiply_add_fusion = f32[3,512,512]{2,1,0:T(8,128)S(1)} fusion(bf16[3,512,512]{2,1,0:T(8,128)(2,1)} %copy-done, bf16[3,6,512]{2,1,0:T(8,128)(2,1)S(1)} %collective-permute-done, f32[3,512]{1,0:T(4,128)S(1)} %get-tuple-element.402, f32[3,512]{1,0:T(4,128)S(1)} %get-tuple-element.403, f32[3,512]{1,0:T(4,128)S(1)} %get-tuple-element.404, ...), kind=kLoop, calls=%fused_computation.40 | loop fusion | flops 29884416 | bytes 4780032 | tf_op jit(solution)/shard_map/add | solution.py:19
  222.1 42.4 %while.42 = (s32[]{:T(128)}, f32[16,512]{1,0:T(8,128)S(1)}, f32[8,64,512]{2,1,0:T(8,128)}, s32[8,64]{1,0:T(8,128)S(1)}, bf16[8,64,512]{2,1,0:T(8,128)(2,1)}, /*i...) while((s32[]{:T(128)}, f32[16,512]{1,0:T(8,128)S(1)}, ...), condition=%wide.region_6.7_spmd.clone.clone, body=%wide.region_3.6_spmd.clone.clone.sunk | while | flops 406872128 | bytes 7376273 | solution.py:55
  223.6 3.1 multiply_reduce_fusion.5
  228.9 3.1 multiply_reduce_fusion.5
  234.2 3.1 multiply_reduce_fusion.5
  239.5 3.1 multiply_reduce_fusion.5
  244.8 3.1 multiply_reduce_fusion.5
  250.1 3.1 multiply_reduce_fusion.5
  255.4 3.1 multiply_reduce_fusion.5
  260.7 3.1 multiply_reduce_fusion.5
  265.2 61.6 %all-gather.7.cloned.1.call-done = f32[512,512]{1,0:T(8,128)} async-done(((f32[16,512]{1,0:T(8,128)}), f32[512,512]{1,0:T(8,128)}) %all-gather.7.cloned.1.call-update) | async-done | bytes 1048592 | tf_op jit(solution)/shard_map/all_gather | solution.py:113
  326.7 26.0 %while.41 = (s32[]{:T(128)}, f32[16,512]{1,0:T(8,128)S(1)}, s32[]{:T(128)}, f32[32,16,512]{2,1,0:T(8,128)}, f32[32,16,512]{2,1,0:T(8,128)}, /*index=5*/s32[]{:T(128)}, s32[]{:T(128)}) while((s32[]{:T(128)}, f32[16,512]{1,0:T(8,128)S(1)}, s32[]{:T(128)}, f32[32,16,512]{2,1,0:T(8,128)}, f32[32,16,512]{2,1,0:T(8,128)}, ...), condition=%wide.region_9.10_spmd.clone, body=%wide.region_8.9_spmd.clone.sunk | while | flops 32772 | bytes 131181 | solution.py:121
  353.9 10.9 %while.40 = (s32[]{:T(128)}, f32[8,64,512]{2,1,0:T(8,128)}, f32[8,64]{1,0:T(8,128)S(1)}, f32[16,512]{1,0:T(8,128)S(1)}, f32[8,64]{1,0:T(8,128)S(1)}, /*index=5*/f32[16,512]{1,0:T(8,128)S(1)}, s32[]{:T(128)}) while((s32[]{:T(128)}, f32[8,64,512]{2,1,0:T(8,128)}, f32[8,64]{1,0:T(8,128)S(1)}, f32[16,512]{1,0:T(8,128)S(1)}, ...), condition=%wide.region_12.13_spmd, body=%wide.region_10.12_spmd.sunk | while | flops 1572930 | bytes 460381 | solution.py:81
  364.7 1.8 add.110
  (201 shorter events, 65.0 us)
Async XLA Ops:
  80.5 17.9 %copy-start.5 = (s32[512]{0:T(512)S(1)}, s32[512]{0:T(512)}, u32[]{:S(2)}) copy-start(s32[512]{0:T(512)} %param.15) | copy-start | bytes 6148
  80.5 19.2 %copy-start.2 = (f32[16,512]{1,0:T(8,128)S(1)}, f32[16,512]{1,0:T(8,128)}, u32[]{:S(2)}) copy-start(f32[16,512]{1,0:T(8,128)} %param.17) | copy-start | bytes 98308
  80.5 19.2 %copy-start.4 = (f32[16,512]{1,0:T(8,128)S(1)}, f32[16,512]{1,0:T(8,128)}, u32[]{:S(2)}) copy-start(f32[16,512]{1,0:T(8,128)} %param.18) | copy-start | bytes 98308
  80.5 20.3 %copy-start.7 = (s32[1,32]{1,0:T(1,128)S(1)}, s32[1,32]{1,0:T(1,128)}, u32[]{:S(2)}) copy-start(s32[1,32]{1,0:T(1,128)} %param.14) | copy-start | bytes 388
  80.6 21.0 %copy-start.3 = (f32[3,7,512]{2,1,0:T(8,128)S(1)}, f32[3,7,512]{2,1,0:T(8,128)}, u32[]{:S(2)}) copy-start(f32[3,7,512]{2,1,0:T(8,128)} %param.16) | copy-start | bytes 129028
  80.6 121.8 %all-to-all-start.1 = ((bf16[3,512,512]{2,0,1:T(4,128)(2,1)}), bf16[3,512,512]{2,0,1:T(4,128)(2,1)S(1)}, u32[]{:S(2)}, u32[]{:S(2)}) async-start(bf16[3,512,512]{2,0,1:T(4,128)(2,1)} %copy.28), calls=%async_computation.1 | async-start | bytes 4194304 | tf_op jit(solution)/shard_map/all_to_all | solution.py:87
  98.4 166.8 %all-gather.5.cloned.1.call-start = ((), (), s32[]{:S(2)}) async-start(), calls=%async_computation.2 | async-start | bytes 1081344 | tf_op jit(solution)/shard_map/all_gather | solution.py:112
  100.4 226.4 %all-gather.7.cloned.1.call-start = ((), (), s32[]{:S(2)}) async-start(), calls=%async_computation.3 | async-start | bytes 1081344 | tf_op jit(solution)/shard_map/all_gather | solution.py:113
  206.4 1.2 copy-start
  207.6 5.5 %collective-permute-start = (bf16[3,6,512]{2,1,0:T(8,128)(2,1)S(1)}, bf16[3,6,512]{2,1,0:T(8,128)(2,1)S(1)}, u32[]{:S(2)}, u32[]{:S(2)}) collective-permute-start(bf16[3,6,512]{2,1,0:T(8,128)(2,1)S(1)} %slice.87), channel_id=1, source_target_pairs={{0,16},{16,32},{32,48},{48,64},{64,80},{80,96},{96,112},{112,128},... | collective-permute-start | bytes 55304 | tf_op jit(solution)/shard_map/ppermute | solution.py:10
  264.5 0.6 copy-start.1
  364.7 1.8 copy-start.6
Sparse Core Ops, SparseCore 0:
  101.3 93.4 all-gather.4
  265.3 61.4 all-gather.6
where the time goes:
time: 378 us; the launch traced here: 375 us
  waiting for transfers between devices  163 us (43%)
  local copies, waits for them, and re-layouts  60.3 us (16%)
  other arithmetic  59.9 us (16%)
  blocking collectives  28.7 us (8%)
  matrix products  24.7 us (7%)
  starting transfers between devices  22.6 us (6%)
  between operations  14.3 us (4%)
    all_to_all x1, waiting for transfers between devices, on_device(): lax.all_to_all(lax.all_to_all(arrived, 'chan', split_axis=2, concat_axis=...  101 us
    all_gather x1, waiting for transfers between devices, on_device(): lax.all_gather(end_state[None], 'seq', axis=0, tiled=True)  61.6 us
    unnamed x23, local copies, waits for them, and re-layouts  33.9 us
    all_to_all x1, blocking collectives, on_device(): lax.all_to_all(arrived, 'chan', split_axis=2, concat_axis=1, tiled=True)  28.7 us
    select_n x32, other arithmetic, absorb(): return jnp.where(shard_idx < position, updated, carried_state)  25.2 us
    dot_general x8, matrix products, advance(): jnp.dot(same_doc, lifted, precision=lax.Precision.HIGHEST)  24.7 us
    all_to_all x1, starting transfers between devices, on_device(): lax.all_to_all(lax.all_to_all(arrived, 'chan', split_axis=2, concat_axis=...  17.8 us
    all_to_all x2, local copies, waits for them, and re-layouts, on_device(): lax.all_to_all(arrived, 'chan', split_axis=2, concat_axis=1, tiled=True)  13.2 us
  transfers between devices with their start and end apart: 4, of which 3 were waited for; matrix products, arithmetic and copies ran while one was open for 15% of the time, Pallas kernels for 0%

commit v1 on v0

v1 whole, which is shorter than its diff:
```python
import jax
import jax.numpy as jnp
from jax import lax
from jax.experimental import pallas as pl
from jax.experimental.pallas import tpu as pltpu
from jax.sharding import PartitionSpec as P

MESH = pl.DeviceIdType.MESH
ORDERED = (1, 2, 0)
F32 = jnp.float32
BF16 = jnp.bfloat16


def one_minus_exp(u):
    series = jnp.ones_like(u)
    for k in range(10, 1, -1):
        series = 1.0 - (u * (1.0 / k)) * series
    return jnp.where(u < 0.5, u * series, 1.0 - jnp.exp(-u))


def kernel(
    a_ref, land_ref, reset_ref, taps_ref, rate_ref, resid_ref, skip_ref, out_ref,
    mid, buf0, buf1, buf2, hsend, hrecv, ext, gated, modal, res, keep, step_decay, weight, enter, through,
    ends, msg0, sib, l1buf, l2buf, entering, src,
    p1s, p1r, zs, zr, hs, hr, l0s, l0r, l1s, l1r, l2s, l2r,
):
    q = lax.axis_index("seq")
    c = lax.axis_index("chan")
    z = q // 2
    core = q % 2
    group, member = z // 4, z % 4

    def remote(source, target, device, send, recv):
        return pltpu.make_async_remote_copy(
            src_ref=source, dst_ref=target, send_sem=send, recv_sem=recv,
            device_id=device, device_id_type=MESH,
        )

    barrier = pltpu.get_barrier_semaphore()

    @pl.loop(1, 16)
    def _(i):
        pl.semaphore_signal(barrier, inc=1, device_id=(q, lax.rem(c + i, 16)), device_id_type=MESH)

    @pl.loop(1, 32)
    def _(i):
        pl.semaphore_signal(barrier, inc=1, device_id=(lax.rem(q + i, 32), c), device_id_type=MESH)

    pl.semaphore_wait(barrier, 46)

    buf = (buf0, buf1, buf2)

    def columns(dc):
        return pl.ds(pl.multiple_of(dc * 512, 512), 512)

    def shift_at(j):
        return lax.rem(j - 1 + z, 15) + 1

    def plane_send(f, j):
        dc = lax.rem(c + 16 - shift_at(j), 16)
        remote(a_ref.at[f, :, columns(dc)], mid.at[f, j - 1], (q, dc), p1s, p1r.at[f, j - 1]).start()

    def forward(f, block, target_z):
        for k in range(2):
            to = 2 * target_z + k
            rows = block.at[pl.ds(16 * k, 16)]

            @pl.when(to == q)
            def _():
                pltpu.make_async_copy(rows, buf[f].at[q], zr.at[f]).start()

            @pl.when(to != q)
            def _():
                remote(rows, buf[f].at[q], (to, c), zs.at[f], zr.at[f]).start()

    first = ORDERED[0]

    @pl.loop(1, 16)
    def _(j):
        plane_send(first, j)

    @pl.loop(0, 32)
    def _(k):
        total = jnp.int32(0)
        for s in range(32):
            total = jnp.where(land_ref[0, s] == k, jnp.int32(s), total)
        src[k] = total

    for at, f in enumerate(ORDERED):
        if at == 2:
            remote(buf[first].at[pl.ds(0, 31)], buf[first].at[pl.ds(0, 31)], (q, c), zs.at[first], zr.at[first]).wait_send()
        forward(f, a_ref.at[f, :, columns(c)], c)

        @pl.loop(1, 16)
        def _(j, f=f, at=at):
            remote(mid.at[f, j - 1], mid.at[f, j - 1], (q, c), p1s, p1r.at[f, j - 1]).wait_recv()
            forward(f, mid.at[f, j - 1], lax.rem(c + shift_at(j), 16))
            if at < 2:
                plane_send(ORDERED[at + 1], j)

        if at == 0:
            sub = lax.broadcasted_iota(jnp.int32, (8, 128), 0)

            @pl.loop(0, 64)
            def _(t):
                marks = jnp.zeros((8, 128), jnp.int32)
                for i in range(8):
                    marks = jnp.where(sub == i, reset_ref[64 * i + t], marks)
                keep[t] = (1 - marks).astype(F32)

            for l in range(4):
                lanes = pl.ds(128 * l, 128)
                rate = rate_ref[:, lanes]
                decay = jnp.exp(-rate)
                gain = resid_ref[:, lanes] * jnp.sqrt(one_minus_exp(2.0 * rate))
                step_decay[l] = jnp.broadcast_to(decay[:, None, :], (16, 8, 128))
                weight[l] = jnp.broadcast_to(gain[:, None, :], (16, 8, 128))

    sub = lax.broadcasted_iota(jnp.int32, (8, 128), 0)

    def arrived_set(f):
        remote(buf[f], buf[f], (q, c), zs.at[f], zr.at[f]).wait_recv()
        hsend[f] = buf[f][src[31]]
        remote(hsend.at[f], hrecv.at[f], (lax.rem(q + 1, 32), c), hs.at[f], hr.at[f]).start()

        @pl.loop(0, 32)
        def _(k):
            at_row = pl.multiple_of(8 + 16 * k, 8)
            for l in range(4):
                ext[f, l, pl.ds(at_row, 16), :] = buf[f][src[k], :, pl.ds(128 * l, 128)].astype(F32)

    def border(f):
        remote(hsend.at[f], hrecv.at[f], (q, c), hs.at[f], hr.at[f]).wait()
        for l in range(4):
            tail = hrecv[f, :, pl.ds(128 * l, 128)].astype(F32)[8:16]
            ext[f, l, pl.ds(0, 8), :] = jnp.where(q == 0, jnp.zeros_like(tail), tail)

    def conv(f, l, tb):
        first_row = 2 + 8 * tb
        window = jnp.stack([ext[f, l, pl.ds(first_row + m, 8, stride=64), :] for m in range(14)])
        total = taps_ref[f, pl.ds(0, 1), pl.ds(128 * l, 128)][None] * window[6:14]
        for j in range(1, 7):
            total = total + taps_ref[f, pl.ds(j, 1), pl.ds(128 * l, 128)][None] * window[6 - j : 14 - j]
        return total

    def gate(tb):
        for l in range(4):
            product = conv(1, l, tb) * conv(2, l, tb)
            gated[l, pl.ds(8 * tb, 8)] = product.astype(BF16).astype(F32)

    arrived_set(1)
    arrived_set(2)

    @pl.loop(1, 8)
    def _(tb):
        gate(tb)

    border(1)
    border(2)
    gate(0)

    kept = lax.fori_loop(0, 64, lambda t, v: v * keep[t], jnp.ones((8, 128), F32))

    @pl.loop(0, 4)
    def _(l):
        skip = skip_ref[l]

        def advance(t, states):
            value = gated[l, t]
            states = states * (step_decay[l] * keep[t][None]) + value[None]
            modal[l, t] = skip * value + jnp.sum(weight[l] * states, axis=0)
            return states

        states = lax.fori_loop(0, 64, advance, jnp.zeros((16, 8, 128), F32))
        power = step_decay[l]
        for _ in range(6):
            power = power * power
        for n in range(16):
            a, b = power[n] * kept, states[n]
            for by in (1, 2, 4):
                a_before = jnp.where(sub < by, 1.0, pltpu.roll(a, by, 0))
                b_before = jnp.where(sub < by, 0.0, pltpu.roll(b, by, 0))
                b = b + a * b_before
                a = a * a_before
            ends[l, pl.ds(n, 1), :] = b[7:8]
            enter[l, n] = jnp.where(sub < 1, 0.0, pltpu.roll(b, 1, 0))
            through[l, n] = jnp.where(sub < 1, 1.0, pltpu.roll(a, 1, 0))

    unbroken = kept
    for by in (4, 2, 1):
        unbroken = unbroken * pltpu.roll(unbroken, by, 0)
    whole_flag = jnp.concatenate([unbroken, unbroken], axis=0)

    for l in range(4):
        msg0[:, pl.ds(128 * l, 128)] = ends[l].astype(BF16)
    msg0[:, pl.ds(512, 128)] = whole_flag.astype(BF16)
    pair = remote(msg0, sib, (q + 1 - 2 * core, c), l0s, l0r)
    pair.start()
    pair.wait()
    flag_lanes = pl.ds(512, 128)
    own_flag = whole_flag
    sib_flag = sib[:, flag_lanes].astype(F32)
    low = core == 0
    flag0 = jnp.where(low, own_flag, sib_flag)
    flag1 = jnp.where(low, sib_flag, own_flag)

    def rates(l, count):
        return jnp.exp(rate_ref[:, pl.ds(128 * l, 128)] * (-float(count)))

    for l in range(4):
        lanes = pl.ds(128 * l, 128)
        own, other = ends[l], sib[:, lanes].astype(F32)
        end0, end1 = jnp.where(low, own, other), jnp.where(low, other, own)
        l1buf[member, :, lanes] = (end1 + rates(l, 512) * flag1 * end0).astype(BF16)
    l1buf[member, :, flag_lanes] = (flag0 * flag1).astype(BF16)

    for o in range(1, 4):
        to = 2 * (4 * group + lax.rem(member + o, 4)) + core
        remote(l1buf.at[member], l1buf.at[member], (to, c), l1s, l1r).start()
    remote(l1buf.at[pl.ds(0, 3)], l1buf.at[pl.ds(0, 3)], (q, c), l1s, l1r).wait()

    def combine(table, mine, l, count):
        lanes = pl.ds(128 * l, 128)
        power = rates(l, count)
        total = jnp.zeros((16, 128), F32)
        before = jnp.zeros((16, 128), F32)
        passed = jnp.ones((16, 128), F32)
        for i in range(4):
            end = table[i, :, lanes].astype(F32)
            factor = power * table[i, :, flag_lanes].astype(F32)
            earlier = mine > i
            before = jnp.where(earlier, before * factor + end, before)
            passed = jnp.where(earlier, passed * factor, passed)
            total = total * factor + end
        return before, passed, total

    for l in range(4):
        before, passed, total = combine(l1buf, member, l, 1024)
        l2buf[group, :, pl.ds(128 * l, 128)] = total.astype(BF16)
        ends_at = before
        entering[0, l] = ends_at
        entering[1, l] = passed
    flags = l1buf[0, :, flag_lanes] * l1buf[1, :, flag_lanes] * l1buf[2, :, flag_lanes] * l1buf[3, :, flag_lanes]
    l2buf[group, :, flag_lanes] = flags

    for o in range(1, 4):
        to = 2 * (4 * lax.rem(group + o, 4) + member) + core
        remote(l2buf.at[group], l2buf.at[group], (to, c), l2s, l2r).start()
    remote(l2buf.at[pl.ds(0, 3)], l2buf.at[pl.ds(0, 3)], (q, c), l2s, l2r).wait()

    for l in range(4):
        lanes = pl.ds(128 * l, 128)
        before, _, _ = combine(l2buf, group, l, 4096)
        into_chip = entering[0, l] + entering[1, l] * before
        after_core0 = sib[:, lanes].astype(F32) + rates(l, 512) * sib_flag * into_chip
        entering[2, l] = jnp.where(low, into_chip, after_core0)

    @pl.loop(0, 4)
    def _(l):
        into = entering[2, l][:, None, :]
        start = weight[l] * (enter[l] + through[l] * into)

        def carry_on(t, states):
            states = states * (step_decay[l] * keep[t][None])
            modal[l, t] = modal[l, t] + jnp.sum(states, axis=0)
            return states

        lax.fori_loop(0, 64, carry_on, start)

    def finish(tb):
        for l in range(4):
            mixed = conv(0, l, tb) * modal[l, pl.ds(8 * tb, 8)]
            for u in range(8):
                res[l, pl.ds(8 * tb + u, 8, stride=64), :] = mixed[u]

    arrived_set(0)

    @pl.loop(1, 8)
    def _(tb):
        finish(tb)

    border(0)
    finish(0)

    @pl.loop(0, 32)
    def _(k):
        rows = pl.ds(pl.multiple_of(16 * k, 16), 16)
        for l in range(4):
            out_ref[rows, pl.ds(128 * l, 128)] = res[l, rows, :].astype(BF16)

    remote(mid, mid, (q, c), p1s, p1r.at[0, 0]).wait_send()
    for f in (2, 0):
        remote(buf[f].at[pl.ds(0, 31)], buf[f].at[pl.ds(0, 31)], (q, c), zs.at[f], zr.at[f]).wait_send()


def on_device(arrived, landing, resets, short_taps, decay_rate, residues, skip_gain):
    skip = jnp.broadcast_to(skip_gain.reshape(4, 1, 128), (4, 8, 128))
    vmem = pl.BlockSpec(memory_space=pltpu.VMEM)
    smem = pl.BlockSpec(memory_space=pltpu.SMEM)
    dma = pltpu.SemaphoreType.DMA
    return pl.pallas_call(
        kernel,
        out_shape=jax.ShapeDtypeStruct((512, 512), BF16),
        in_specs=[pl.BlockSpec(memory_space=pl.ANY), smem, smem, vmem, vmem, vmem, vmem],
        out_specs=vmem,
        scratch_shapes=[
            pltpu.VMEM((3, 15, 32, 512), BF16),
            pltpu.VMEM((32, 16, 512), BF16),
            pltpu.VMEM((32, 16, 512), BF16),
            pltpu.VMEM((32, 16, 512), BF16),
            pltpu.VMEM((3, 16, 512), BF16),
            pltpu.VMEM((3, 16, 512), BF16),
            pltpu.VMEM((3, 4, 520, 128), F32),
            pltpu.VMEM((4, 64, 8, 128), F32),
            pltpu.VMEM((4, 64, 8, 128), F32),
            pltpu.VMEM((4, 512, 128), F32),
            pltpu.VMEM((64, 8, 128), F32),
            pltpu.VMEM((4, 16, 8, 128), F32),
            pltpu.VMEM((4, 16, 8, 128), F32),
            pltpu.VMEM((4, 16, 8, 128), F32),
            pltpu.VMEM((4, 16, 8, 128), F32),
            pltpu.VMEM((4, 16, 128), F32),
            pltpu.VMEM((16, 640), BF16),
            pltpu.VMEM((16, 640), BF16),
            pltpu.VMEM((4, 16, 640), BF16),
            pltpu.VMEM((4, 16, 640), BF16),
            pltpu.VMEM((3, 4, 16, 128), F32),
            pltpu.SMEM((32,), jnp.int32),
            dma, dma((3, 15)), dma((3,)), dma((3,)), dma((3,)), dma((3,)),
            dma, dma, dma, dma, dma, dma,
        ],
        compiler_params=pltpu.CompilerParams(
            collective_id=0, has_side_effects=True, vmem_limit_bytes=40 << 20
        ),
        cost_estimate=pl.CostEstimate(flops=64 << 20, bytes_accessed=4 << 20, transcendentals=1 << 15),
    )(arrived, landing, resets, short_taps, decay_rate, residues, skip)


def solution(mesh):
    in_specs = (
        P(None, ("seq", "chan"), None),
        P("seq", None),
        P("seq"),
        P(None, None, "chan"),
        P(None, "chan"),
        P(None, "chan"),
        P("chan"),
    )
    return jax.shard_map(
        on_device, mesh=mesh, in_specs=in_specs, out_specs=P("seq", "chan"), check_vma=False
    )
```

time: 378 us -> 127 us (0.34)
  the two profiles are of different devices: /device:TPU:1 before, /device:TPU:14 now
where the time goes in v1:
time: 127 us
  Pallas kernels  121 us (95%)
  local copies, waits for them, and re-layouts  6.53 us (5%)
    pallas_call x1, Pallas kernels, on_device(): pl.pallas_call(kernel, out_shape=jax.ShapeDtypeStruct((512, 512), BF16),...  121 us
    unnamed x13, local copies, waits for them, and re-layouts  5.85 us

profile of v1, /device:TPU:14, one launch (start us, length us, event | category | flops | bytes accessed | tf_op | source)
XLA Modules:
  0.0 127.1 jit_solution(3298495664149659666)
XLA Ops:
  0.0 0.7 broadcast_in_dim.8.skip_ref
  0.7 0.0 copy-start
  0.7 1.4 %copy-done = bf16[3,32,8192]{2,1,0:T(8,128)(2,1)S(1)} copy-done((bf16[3,32,8192]{2,1,0:T(8,128)(2,1)S(1)}, bf16[3,32,8192]{2,1,0:T(8,128)(2,1)}, u32[]{:S(2)}) %copy-start) | copy-done | bytes 1572888
  2.1 0.0 copy-start.1
  2.1 0.8 copy-done.1
  2.9 0.0 copy-start.2
  2.9 0.8 copy-done.2
  3.6 0.0 copy-start.3
  3.7 0.8 copy-done.3
  4.4 0.0 copy-start.4
  4.4 0.7 copy-done.4
  5.1 0.0 copy-start.5
  5.1 0.7 copy-done.5
  5.7 120.5 %shard_map.73 = bf16[512,512]{1,0:T(8,128)(2,1)S(1)} custom-call(bf16[3,32,8192]{2,1,0:T(8,128)(2,1)S(1)} %copy-done, s32[1,32]{1,0:T(1,128)S(1)} %copy-done.5, s32[512]{0:T(512)S(1)} %copy-done.4, f32[3,7,512]{2,1,0:T(8,128)S(1)} %copy-done.1, f32[16,512]{1,0:T(8,128)S(1)} %copy-done.2, f32[16,512]{1,0:T(8,128)S(1)} %copy-done.3, ...), custom_call_target="tpu_custom_call" | custom-call | flops 67108864 | bytes 4194304 | tf_op jit(solution)/shard_map/pallas_call | solution.py:301
  126.3 0.8 copy.9
Async XLA Ops:
  0.7 1.4 %copy-start = (bf16[3,32,8192]{2,1,0:T(8,128)(2,1)S(1)}, bf16[3,32,8192]{2,1,0:T(8,128)(2,1)}, u32[]{:S(2)}) copy-start(bf16[3,32,8192]{2,1,0:T(8,128)(2,1)} %a_ref.1) | copy-start | bytes 4718596
  2.1 0.8 copy-start.1
  2.9 0.8 copy-start.2
  3.6 0.8 copy-start.3
  4.4 0.7 copy-start.4
  5.1 0.7 copy-start.5

commit v2 on v1

v2 whole, which is shorter than its diff:
```python
import jax
import jax.numpy as jnp
from jax import lax
from jax.experimental import pallas as pl
from jax.experimental.pallas import tpu as pltpu
from jax.sharding import PartitionSpec as P

MESH = pl.DeviceIdType.MESH
HALF = 256
PIECES = ((1, 0), (2, 0), (1, 1), (2, 1), (0, 0), (0, 1))
UNROLL = 4
F32 = jnp.float32
BF16 = jnp.bfloat16


def one_minus_exp(u):
    series = jnp.ones_like(u)
    for k in range(10, 1, -1):
        series = 1.0 - (u * (1.0 / k)) * series
    return jnp.where(u < 0.5, u * series, 1.0 - jnp.exp(-u))


def kernel(
    a_ref, land_ref, reset_ref, taps_ref, rate_ref, resid_ref, skip_ref, out_ref,
    mid, buf0, buf1, buf2, buf3, buf4, buf5, hsend, hrecv, ext, gated, modal, res, keep, step_decay, weight, enter, through,
    ends, msg0, sib, l1buf, l2buf, entering, src,
    p1s, p1r, zs, zr, hs, hr, l0s, l0r, l1s, l1r, l2s, l2r, far,
):
    q = lax.axis_index("seq")
    c = lax.axis_index("chan")
    z = q // 2
    core = q % 2
    group, member = z // 4, z % 4

    def remote(source, target, device, send, recv):
        return pltpu.make_async_remote_copy(
            src_ref=source, dst_ref=target, send_sem=send, recv_sem=recv,
            device_id=device, device_id_type=MESH,
        )

    barrier = pltpu.get_barrier_semaphore()

    def greet(device):
        pl.semaphore_signal(barrier, inc=1, device_id=device, device_id_type=MESH)

    @pl.loop(1, 16)
    def _(i):
        greet((q, lax.rem(c + i, 16)))

    @pl.loop(1, 5)
    def _(i):
        for k in range(2):
            greet((2 * lax.rem(z + i, 16) + k, c))
            greet((2 * lax.rem(z + 16 - i, 16) + k, c))

    greet((q + 1 - 2 * core, c))
    pl.semaphore_wait(barrier, 32)
    for beyond in (8, 24):
        pl.semaphore_signal(far, inc=1, device_id=(lax.rem(q + beyond, 32), c), device_id_type=MESH)

    buf = (buf0, buf1, buf2, buf3, buf4, buf5)

    def columns(dc, half):
        return pl.ds(pl.multiple_of(dc * 512 + half * HALF, 128), HALF)

    def shift_at(j):
        return lax.rem(j - 1 + z, 15) + 1

    def plane_send(p, j):
        f, half = PIECES[p]
        dc = lax.rem(c + 16 - shift_at(j), 16)
        remote(a_ref.at[f, :, columns(dc, half)], mid.at[p, j - 1], (q, dc), p1s, p1r.at[p, j - 1]).start()

    def ring_send(p, block, target_z):
        for k in range(2):
            to = 2 * target_z + k
            rows = block.at[pl.ds(16 * k, 16)]

            @pl.when(to == q)
            def _():
                pltpu.make_async_copy(rows, buf[p].at[q], zr.at[p]).start()

            @pl.when(to != q)
            def _():
                remote(rows, buf[p].at[q], (to, c), zs.at[p], zr.at[p]).start()

    def forward(p, first=0, stop=16):
        f, half = PIECES[p]
        if first == 0:
            ring_send(p, a_ref.at[f, :, columns(c, half)], c)

        @pl.loop(max(first, 1), stop)
        def _(j):
            remote(mid.at[p, j - 1], mid.at[p, j - 1], (q, c), p1s, p1r.at[p, j - 1]).wait_recv()
            ring_send(p, mid.at[p, j - 1], lax.rem(c + shift_at(j), 16))
            if p + 1 < len(PIECES):
                plane_send(p + 1, j)

    @pl.loop(1, 16)
    def _(j):
        plane_send(0, j)

    @pl.loop(0, 32)
    def _(k):
        total = jnp.int32(0)
        for s in range(32):
            total = jnp.where(land_ref[0, s] == k, jnp.int32(s), total)
        src[k] = total

    pl.semaphore_wait(far, 2)
    forward(0)

    sub = lax.broadcasted_iota(jnp.int32, (8, 128), 0)

    @pl.loop(0, 64)
    def _(t):
        marks = jnp.zeros((8, 128), jnp.int32)
        for i in range(8):
            marks = jnp.where(sub == i, reset_ref[64 * i + t], marks)
        keep[t] = (1 - marks).astype(F32)

    for l in range(4):
        lanes = pl.ds(128 * l, 128)
        rate = rate_ref[:, lanes]
        decay = jnp.exp(-rate)
        gain = resid_ref[:, lanes] * jnp.sqrt(one_minus_exp(2.0 * rate))
        step_decay[l] = jnp.broadcast_to(decay[:, None, :], (16, 8, 128))
        weight[l] = jnp.broadcast_to(gain[:, None, :], (16, 8, 128))

    kept = lax.fori_loop(0, 64, lambda t, v: v * keep[t], jnp.ones((8, 128), F32))

    for p in (1, 2, 3):
        forward(p)

    def sum16(v):
        v = v[:8] + v[8:]
        v = v[:4] + v[4:]
        v = v[:2] + v[2:]
        return v[0] + v[1]

    def arrived_piece(p):
        f, half = PIECES[p]
        remote(buf[p], buf[p], (q, c), zs.at[p], zr.at[p]).wait_recv()
        hsend[p] = buf[p][src[31]]
        remote(hsend.at[p], hrecv.at[p], (lax.rem(q + 1, 32), c), hs.at[p], hr.at[p]).start()

        @pl.loop(0, 32)
        def _(k):
            at_row = pl.multiple_of(8 + 16 * k, 8)
            for i in range(2):
                ext[f, 2 * half + i, pl.ds(at_row, 16), :] = buf[p][src[k], :, pl.ds(128 * i, 128)].astype(F32)

    def border(p):
        f, half = PIECES[p]
        remote(hsend.at[p], hrecv.at[p], (q, c), hs.at[p], hr.at[p]).wait()
        for i in range(2):
            tail = hrecv[p, :, pl.ds(128 * i, 128)].astype(F32)[8:16]
            ext[f, 2 * half + i, pl.ds(0, 8), :] = jnp.where(q == 0, jnp.zeros_like(tail), tail)

    def conv(f, l, tb):
        first_row = 2 + 8 * tb
        window = jnp.stack([ext[f, l, pl.ds(first_row + m, 8, stride=64), :] for m in range(14)])
        total = taps_ref[f, pl.ds(0, 1), pl.ds(128 * l, 128)][None] * window[6:14]
        for j in range(1, 7):
            total = total + taps_ref[f, pl.ds(j, 1), pl.ds(128 * l, 128)][None] * window[6 - j : 14 - j]
        return total

    def gate(l, tb):
        product = conv(1, l, tb) * conv(2, l, tb)
        gated[l, pl.ds(8 * tb, 8)] = product.astype(BF16).astype(F32)

    def scan_lanes(l):
        skip = skip_ref[l]

        def advance(step, states):
            for u in range(UNROLL):
                t = UNROLL * step + u
                value = gated[l, t]
                states = states * (step_decay[l] * keep[t][None]) + value[None]
                modal[l, t] = skip * value + sum16(weight[l] * states)
            return states

        states = lax.fori_loop(0, 64 // UNROLL, advance, jnp.zeros((16, 8, 128), F32))
        power = step_decay[l]
        for _ in range(6):
            power = power * power
        for n in range(16):
            a, b = power[n] * kept, states[n]
            for by in (1, 2, 4):
                a_before = jnp.where(sub < by, 1.0, pltpu.roll(a, by, 0))
                b_before = jnp.where(sub < by, 0.0, pltpu.roll(b, by, 0))
                b = b + a * b_before
                a = a * a_before
            ends[l, pl.ds(n, 1), :] = b[7:8]
            enter[l, n] = jnp.where(sub < 1, 0.0, pltpu.roll(b, 1, 0))
            through[l, n] = jnp.where(sub < 1, 1.0, pltpu.roll(a, 1, 0))

    def gate_and_scan(half):
        lanes = (2 * half, 2 * half + 1)

        @pl.loop(1, 8)
        def _(tb):
            for l in lanes:
                gate(l, tb)

        border(2 * half)
        border(2 * half + 1)
        for l in lanes:
            gate(l, 0)
        pl.loop(lanes[0], lanes[1] + 1)(scan_lanes)

    arrived_piece(0)
    arrived_piece(1)
    gate_and_scan(0)
    forward(4, 0, 6)
    arrived_piece(2)
    arrived_piece(3)
    forward(4, 6, 14)
    gate_and_scan(1)

    unbroken = kept
    for by in (4, 2, 1):
        unbroken = unbroken * pltpu.roll(unbroken, by, 0)
    whole_flag = jnp.concatenate([unbroken, unbroken], axis=0)

    for l in range(4):
        msg0[:, pl.ds(128 * l, 128)] = ends[l].astype(BF16)
    msg0[:, pl.ds(512, 128)] = whole_flag.astype(BF16)
    pair = remote(msg0, sib, (q + 1 - 2 * core, c), l0s, l0r)
    pair.start()
    forward(4, 14, 16)
    pair.wait()
    flag_lanes = pl.ds(512, 128)
    own_flag = whole_flag
    sib_flag = sib[:, flag_lanes].astype(F32)
    low = core == 0
    flag0 = jnp.where(low, own_flag, sib_flag)
    flag1 = jnp.where(low, sib_flag, own_flag)

    def rates(l, count):
        return jnp.exp(rate_ref[:, pl.ds(128 * l, 128)] * (-float(count)))

    for l in range(4):
        lanes = pl.ds(128 * l, 128)
        own, other = ends[l], sib[:, lanes].astype(F32)
        end0, end1 = jnp.where(low, own, other), jnp.where(low, other, own)
        l1buf[member, :, lanes] = (end1 + rates(l, 512) * flag1 * end0).astype(BF16)
    l1buf[member, :, flag_lanes] = (flag0 * flag1).astype(BF16)

    for o in range(1, 4):
        to = 2 * (4 * group + lax.rem(member + o, 4)) + core
        remote(l1buf.at[member], l1buf.at[member], (to, c), l1s, l1r).start()
    forward(5, 0, 8)
    remote(l1buf.at[pl.ds(0, 3)], l1buf.at[pl.ds(0, 3)], (q, c), l1s, l1r).wait()

    def combine(table, mine, l, count):
        lanes = pl.ds(128 * l, 128)
        power = rates(l, count)
        total = jnp.zeros((16, 128), F32)
        before = jnp.zeros((16, 128), F32)
        passed = jnp.ones((16, 128), F32)
        for i in range(4):
            end = table[i, :, lanes].astype(F32)
            factor = power * table[i, :, flag_lanes].astype(F32)
            earlier = mine > i
            before = jnp.where(earlier, before * factor + end, before)
            passed = jnp.where(earlier, passed * factor, passed)
            total = total * factor + end
        return before, passed, total

    for l in range(4):
        before, passed, total = combine(l1buf, member, l, 1024)
        l2buf[group, :, pl.ds(128 * l, 128)] = total.astype(BF16)
        ends_at = before
        entering[0, l] = ends_at
        entering[1, l] = passed
    flags = l1buf[0, :, flag_lanes] * l1buf[1, :, flag_lanes] * l1buf[2, :, flag_lanes] * l1buf[3, :, flag_lanes]
    l2buf[group, :, flag_lanes] = flags

    for o in range(1, 4):
        to = 2 * (4 * lax.rem(group + o, 4) + member) + core
        remote(l2buf.at[group], l2buf.at[group], (to, c), l2s, l2r).start()
    forward(5, 8, 16)
    remote(l2buf.at[pl.ds(0, 3)], l2buf.at[pl.ds(0, 3)], (q, c), l2s, l2r).wait()

    for l in range(4):
        lanes = pl.ds(128 * l, 128)
        before, _, _ = combine(l2buf, group, l, 4096)
        into_chip = entering[0, l] + entering[1, l] * before
        after_core0 = sib[:, lanes].astype(F32) + rates(l, 512) * sib_flag * into_chip
        entering[2, l] = jnp.where(low, into_chip, after_core0)

    @pl.loop(0, 4)
    def _(l):
        into = entering[2, l][:, None, :]
        start = weight[l] * (enter[l] + through[l] * into)

        def carry_on(step, carried):
            states, held = carried
            for u in range(UNROLL):
                t = UNROLL * step + u
                held = held * keep[t]
                states = states * step_decay[l]
                modal[l, t] = modal[l, t] + held * sum16(states)
            return states, held

        lax.fori_loop(0, 64 // UNROLL, carry_on, (start, jnp.ones((8, 128), F32)))

    def finish(l, tb):
        mixed = conv(0, l, tb) * modal[l, pl.ds(8 * tb, 8)]
        for u in range(8):
            res[l, pl.ds(8 * tb + u, 8, stride=64), :] = mixed[u]

    for half in range(2):
        lanes = (2 * half, 2 * half + 1)
        arrived_piece(4 + half)

        @pl.loop(1, 8)
        def _(tb):
            for l in lanes:
                finish(l, tb)

        border(4 + half)
        for l in lanes:
            finish(l, 0)

        @pl.loop(0, 32)
        def _(k):
            rows = pl.ds(pl.multiple_of(16 * k, 16), 16)
            for l in lanes:
                out_ref[rows, pl.ds(128 * l, 128)] = res[l, rows, :].astype(BF16)

    remote(mid, mid, (q, c), p1s, p1r.at[0, 0]).wait_send()
    for p in range(len(PIECES)):
        gone = buf[p].at[pl.ds(0, 31)]
        remote(gone, gone, (q, c), zs.at[p], zr.at[p]).wait_send()


def on_device(arrived, landing, resets, short_taps, decay_rate, residues, skip_gain):
    skip = jnp.broadcast_to(skip_gain.reshape(4, 1, 128), (4, 8, 128))
    vmem = pl.BlockSpec(memory_space=pltpu.VMEM)
    smem = pl.BlockSpec(memory_space=pltpu.SMEM)
    dma = pltpu.SemaphoreType.DMA
    return pl.pallas_call(
        kernel,
        out_shape=jax.ShapeDtypeStruct((512, 512), BF16),
        in_specs=[pl.BlockSpec(memory_space=pl.ANY), smem, smem, vmem, vmem, vmem, vmem],
        out_specs=vmem,
        scratch_shapes=[
            pltpu.VMEM((6, 15, 32, HALF), BF16),
            *[pltpu.VMEM((32, 16, HALF), BF16)] * 6,
            pltpu.VMEM((6, 16, HALF), BF16),
            pltpu.VMEM((6, 16, HALF), BF16),
            pltpu.VMEM((3, 4, 520, 128), F32),
            pltpu.VMEM((4, 64, 8, 128), F32),
            pltpu.VMEM((4, 64, 8, 128), F32),
            pltpu.VMEM((4, 512, 128), F32),
            pltpu.VMEM((64, 8, 128), F32),
            pltpu.VMEM((4, 16, 8, 128), F32),
            pltpu.VMEM((4, 16, 8, 128), F32),
            pltpu.VMEM((4, 16, 8, 128), F32),
            pltpu.VMEM((4, 16, 8, 128), F32),
            pltpu.VMEM((4, 16, 128), F32),
            pltpu.VMEM((16, 640), BF16),
            pltpu.VMEM((16, 640), BF16),
            pltpu.VMEM((4, 16, 640), BF16),
            pltpu.VMEM((4, 16, 640), BF16),
            pltpu.VMEM((3, 4, 16, 128), F32),
            pltpu.SMEM((32,), jnp.int32),
            dma, dma((6, 15)), dma((6,)), dma((6,)), dma((6,)), dma((6,)),
            dma, dma, dma, dma, dma, dma, pltpu.SemaphoreType.REGULAR,
        ],
        compiler_params=pltpu.CompilerParams(
            collective_id=0, has_side_effects=True, vmem_limit_bytes=40 << 20
        ),
        cost_estimate=pl.CostEstimate(flops=64 << 20, bytes_accessed=4 << 20, transcendentals=1 << 15),
    )(arrived, landing, resets, short_taps, decay_rate, residues, skip)


def solution(mesh):
    in_specs = (
        P(None, ("seq", "chan"), None),
        P("seq", None),
        P("seq"),
        P(None, None, "chan"),
        P(None, "chan"),
        P(None, "chan"),
        P("chan"),
    )
    return jax.shard_map(
        on_device, mesh=mesh, in_specs=in_specs, out_specs=P("seq", "chan"), check_vma=False
    )
```

time: 127 us -> 112 us (0.88)
  the two profiles are of different devices: /device:TPU:14 before, /device:TPU:4 now
where the time goes in v2:
time: 112 us
  Pallas kernels  105 us (94%)
  local copies, waits for them, and re-layouts  6.53 us (6%)
    pallas_call x1, Pallas kernels, on_device(): pl.pallas_call(kernel, out_shape=jax.ShapeDtypeStruct((512, 512), BF16),...  105 us
    unnamed x13, local copies, waits for them, and re-layouts  5.85 us

profile of v2, /device:TPU:4, one launch (start us, length us, event | category | flops | bytes accessed | tf_op | source)
XLA Modules:
  0.0 111.6 jit_solution(7232520094921108225)
XLA Ops:
  0.0 0.7 broadcast_in_dim.8.skip_ref
  0.7 0.0 copy-start
  0.7 1.4 %copy-done = bf16[3,32,8192]{2,1,0:T(8,128)(2,1)S(1)} copy-done((bf16[3,32,8192]{2,1,0:T(8,128)(2,1)S(1)}, bf16[3,32,8192]{2,1,0:T(8,128)(2,1)}, u32[]{:S(2)}) %copy-start) | copy-done | bytes 1572888
  2.1 0.0 copy-start.1
  2.1 0.8 copy-done.1
  2.9 0.0 copy-start.2
  2.9 0.8 copy-done.2
  3.6 0.0 copy-start.3
  3.7 0.8 copy-done.3
  4.4 0.0 copy-start.4
  4.4 0.7 copy-done.4
  5.1 0.0 copy-start.5
  5.1 0.7 copy-done.5
  5.7 105.0 %shard_map.73 = bf16[512,512]{1,0:T(8,128)(2,1)S(1)} custom-call(bf16[3,32,8192]{2,1,0:T(8,128)(2,1)S(1)} %copy-done, s32[1,32]{1,0:T(1,128)S(1)} %copy-done.5, s32[512]{0:T(512)S(1)} %copy-done.4, f32[3,7,512]{2,1,0:T(8,128)S(1)} %copy-done.1, f32[16,512]{1,0:T(8,128)S(1)} %copy-done.2, f32[16,512]{1,0:T(8,128)S(1)} %copy-done.3, ...), custom_call_target="tpu_custom_call" | custom-call | flops 67108864 | bytes 4194304 | tf_op jit(solution)/shard_map/pallas_call | solution.py:344
  110.8 0.8 copy.9
Async XLA Ops:
  0.7 1.4 %copy-start = (bf16[3,32,8192]{2,1,0:T(8,128)(2,1)S(1)}, bf16[3,32,8192]{2,1,0:T(8,128)(2,1)}, u32[]{:S(2)}) copy-start(bf16[3,32,8192]{2,1,0:T(8,128)(2,1)} %a_ref.1) | copy-start | bytes 4718596
  2.1 0.8 copy-start.1
  2.9 0.8 copy-start.2
  3.6 0.8 copy-start.3
  4.4 0.7 copy-start.4
  5.1 0.7 copy-start.5

commit v3 on v2

--- a/solution.py
+++ b/solution.py
@@ -6,9 +6,9 @@
 from jax.sharding import PartitionSpec as P
 
 MESH = pl.DeviceIdType.MESH
-HALF = 256
+PARTS = ((0, 2), (2, 2))
 PIECES = ((1, 0), (2, 0), (1, 1), (2, 1), (0, 0), (0, 1))
-UNROLL = 4
+UNROLL = 8
 F32 = jnp.float32
 BF16 = jnp.bfloat16
 
@@ -22,7 +22,8 @@
 
 def kernel(
     a_ref, land_ref, reset_ref, taps_ref, rate_ref, resid_ref, skip_ref, out_ref,
-    mid, buf0, buf1, buf2, buf3, buf4, buf5, hsend, hrecv, ext, gated, modal, res, keep, step_decay, weight, enter, through,
+    mid0, mid1, mid2, mid3, mid4, mid5, buf0, buf1, buf2, buf3, buf4, buf5,
+    hsend0, hsend1, hsend2, hsend3, hsend4, hsend5, hrecv0, hrecv1, hrecv2, hrecv3, hrecv4, hrecv5, ext, gated, modal, res, keep, step_decay, weight, enter, through,
     ends, msg0, sib, l1buf, l2buf, entering, src,
     p1s, p1r, zs, zr, hs, hr, l0s, l0r, l1s, l1r, l2s, l2r, far,
 ):
@@ -58,10 +59,14 @@
     for beyond in (8, 24):
         pl.semaphore_signal(far, inc=1, device_id=(lax.rem(q + beyond, 32), c), device_id_type=MESH)
 
+    mid = (mid0, mid1, mid2, mid3, mid4, mid5)
     buf = (buf0, buf1, buf2, buf3, buf4, buf5)
+    hsend = (hsend0, hsend1, hsend2, hsend3, hsend4, hsend5)
+    hrecv = (hrecv0, hrecv1, hrecv2, hrecv3, hrecv4, hrecv5)
 
     def columns(dc, half):
-        return pl.ds(pl.multiple_of(dc * 512 + half * HALF, 128), HALF)
+        group0, groups = PARTS[half]
+        return pl.ds(pl.multiple_of(dc * 512 + 128 * group0, 128), 128 * groups)
 
     def shift_at(j):
         return lax.rem(j - 1 + z, 15) + 1
@@ -69,7 +74,7 @@
     def plane_send(p, j):
         f, half = PIECES[p]
         dc = lax.rem(c + 16 - shift_at(j), 16)
-        remote(a_ref.at[f, :, columns(dc, half)], mid.at[p, j - 1], (q, dc), p1s, p1r.at[p, j - 1]).start()
+        remote(a_ref.at[f, :, columns(dc, half)], mid[p].at[j - 1], (q, dc), p1s.at[p], p1r.at[p, j - 1]).start()
 
     def ring_send(p, block, target_z):
         for k in range(2):
@@ -91,10 +96,10 @@
 
         @pl.loop(max(first, 1), stop)
         def _(j):
-            remote(mid.at[p, j - 1], mid.at[p, j - 1], (q, c), p1s, p1r.at[p, j - 1]).wait_recv()
-            ring_send(p, mid.at[p, j - 1], lax.rem(c + shift_at(j), 16))
-            if p + 1 < len(PIECES):
-                plane_send(p + 1, j)
+            remote(mid[p].at[j - 1], mid[p].at[j - 1], (q, c), p1s.at[p], p1r.at[p, j - 1]).wait_recv()
+            ring_send(p, mid[p].at[j - 1], lax.rem(c + shift_at(j), 16))
+            for ahead in ((p + 1,) if p < 3 else (4, 5) if p == 3 else ()):
+                plane_send(ahead, j)
 
     @pl.loop(1, 16)
     def _(j):
@@ -141,21 +146,21 @@
     def arrived_piece(p):
         f, half = PIECES[p]
         remote(buf[p], buf[p], (q, c), zs.at[p], zr.at[p]).wait_recv()
-        hsend[p] = buf[p][src[31]]
-        remote(hsend.at[p], hrecv.at[p], (lax.rem(q + 1, 32), c), hs.at[p], hr.at[p]).start()
+        hsend[p][...] = buf[p][src[31]]
+        remote(hsend[p], hrecv[p], (lax.rem(q + 1, 32), c), hs.at[p], hr.at[p]).start()
 
         @pl.loop(0, 32)
         def _(k):
             at_row = pl.multiple_of(8 + 16 * k, 8)
-            for i in range(2):
-                ext[f, 2 * half + i, pl.ds(at_row, 16), :] = buf[p][src[k], :, pl.ds(128 * i, 128)].astype(F32)
+            for i in range(PARTS[half][1]):
+                ext[f, PARTS[half][0] + i, pl.ds(at_row, 16), :] = buf[p][src[k], :, pl.ds(128 * i, 128)].astype(F32)
 
     def border(p):
         f, half = PIECES[p]
-        remote(hsend.at[p], hrecv.at[p], (q, c), hs.at[p], hr.at[p]).wait()
-        for i in range(2):
-            tail = hrecv[p, :, pl.ds(128 * i, 128)].astype(F32)[8:16]
-            ext[f, 2 * half + i, pl.ds(0, 8), :] = jnp.where(q == 0, jnp.zeros_like(tail), tail)
+        remote(hsend[p], hrecv[p], (q, c), hs.at[p], hr.at[p]).wait()
+        for i in range(PARTS[half][1]):
+            tail = hrecv[p][:, pl.ds(128 * i, 128)].astype(F32)[8:16]
+            ext[f, PARTS[half][0] + i, pl.ds(0, 8), :] = jnp.where(q == 0, jnp.zeros_like(tail), tail)
 
     def conv(f, l, tb):
         first_row = 2 + 8 * tb
@@ -196,7 +201,7 @@
             through[l, n] = jnp.where(sub < 1, 1.0, pltpu.roll(a, 1, 0))
 
     def gate_and_scan(half):
-        lanes = (2 * half, 2 * half + 1)
+        lanes = tuple(range(PARTS[half][0], sum(PARTS[half])))
 
         @pl.loop(1, 8)
         def _(tb):
@@ -207,7 +212,7 @@
         border(2 * half + 1)
         for l in lanes:
             gate(l, 0)
-        pl.loop(lanes[0], lanes[1] + 1)(scan_lanes)
+        pl.loop(lanes[0], lanes[-1] + 1)(scan_lanes)
 
     arrived_piece(0)
     arrived_piece(1)
@@ -215,7 +220,7 @@
     forward(4, 0, 6)
     arrived_piece(2)
     arrived_piece(3)
-    forward(4, 6, 14)
+    forward(4, 6, 16)
     gate_and_scan(1)
 
     unbroken = kept
@@ -228,7 +233,6 @@
     msg0[:, pl.ds(512, 128)] = whole_flag.astype(BF16)
     pair = remote(msg0, sib, (q + 1 - 2 * core, c), l0s, l0r)
     pair.start()
-    forward(4, 14, 16)
     pair.wait()
     flag_lanes = pl.ds(512, 128)
     own_flag = whole_flag
@@ -250,7 +254,7 @@
     for o in range(1, 4):
         to = 2 * (4 * group + lax.rem(member + o, 4)) + core
         remote(l1buf.at[member], l1buf.at[member], (to, c), l1s, l1r).start()
-    forward(5, 0, 8)
+    forward(5, 0, 10)
     remote(l1buf.at[pl.ds(0, 3)], l1buf.at[pl.ds(0, 3)], (q, c), l1s, l1r).wait()
 
     def combine(table, mine, l, count):
@@ -280,7 +284,7 @@
     for o in range(1, 4):
         to = 2 * (4 * lax.rem(group + o, 4) + member) + core
         remote(l2buf.at[group], l2buf.at[group], (to, c), l2s, l2r).start()
-    forward(5, 8, 16)
+    forward(5, 10, 16)
     remote(l2buf.at[pl.ds(0, 3)], l2buf.at[pl.ds(0, 3)], (q, c), l2s, l2r).wait()
 
     for l in range(4):
@@ -312,7 +316,7 @@
             res[l, pl.ds(8 * tb + u, 8, stride=64), :] = mixed[u]
 
     for half in range(2):
-        lanes = (2 * half, 2 * half + 1)
+        lanes = tuple(range(PARTS[half][0], sum(PARTS[half])))
         arrived_piece(4 + half)
 
         @pl.loop(1, 8)
@@ -330,10 +334,10 @@
             for l in lanes:
                 out_ref[rows, pl.ds(128 * l, 128)] = res[l, rows, :].astype(BF16)
 
-    remote(mid, mid, (q, c), p1s, p1r.at[0, 0]).wait_send()
     for p in range(len(PIECES)):
         gone = buf[p].at[pl.ds(0, 31)]
         remote(gone, gone, (q, c), zs.at[p], zr.at[p]).wait_send()
+        remote(mid[p], mid[p], (q, c), p1s.at[p], p1r.at[p, 0]).wait_send()
 
 
 def on_device(arrived, landing, resets, short_taps, decay_rate, residues, skip_gain):
@@ -341,16 +345,17 @@
     vmem = pl.BlockSpec(memory_space=pltpu.VMEM)
     smem = pl.BlockSpec(memory_space=pltpu.SMEM)
     dma = pltpu.SemaphoreType.DMA
+    widths = [128 * PARTS[half][1] for _, half in PIECES]
     return pl.pallas_call(
         kernel,
         out_shape=jax.ShapeDtypeStruct((512, 512), BF16),
         in_specs=[pl.BlockSpec(memory_space=pl.ANY), smem, smem, vmem, vmem, vmem, vmem],
         out_specs=vmem,
         scratch_shapes=[
-            pltpu.VMEM((6, 15, 32, HALF), BF16),
-            *[pltpu.VMEM((32, 16, HALF), BF16)] * 6,
-            pltpu.VMEM((6, 16, HALF), BF16),
-            pltpu.VMEM((6, 16, HALF), BF16),
+            *[pltpu.VMEM((15, 32, w), BF16) for w in widths],
+            *[pltpu.VMEM((32, 16, w), BF16) for w in widths],
+            *[pltpu.VMEM((16, w), BF16) for w in widths],
+            *[pltpu.VMEM((16, w), BF16) for w in widths],
             pltpu.VMEM((3, 4, 520, 128), F32),
             pltpu.VMEM((4, 64, 8, 128), F32),
             pltpu.VMEM((4, 64, 8, 128), F32),
@@ -367,7 +372,7 @@
             pltpu.VMEM((4, 16, 640), BF16),
             pltpu.VMEM((3, 4, 16, 128), F32),
             pltpu.SMEM((32,), jnp.int32),
-            dma, dma((6, 15)), dma((6,)), dma((6,)), dma((6,)), dma((6,)),
+            dma((6,)), dma((6, 15)), dma((6,)), dma((6,)), dma((6,)), dma((6,)),
             dma, dma, dma, dma, dma, dma, pltpu.SemaphoreType.REGULAR,
         ],
         compiler_params=pltpu.CompilerParams(

time: 112 us -> 111 us (level)
  the two profiles are of different devices: /device:TPU:4 before, /device:TPU:1 now
where the time goes in v3:
time: 111 us; the launch traced here: 109 us
  Pallas kernels  103 us (93%)
  local copies, waits for them, and re-layouts  6.53 us (6%)
    pallas_call x1, Pallas kernels, on_device(): pl.pallas_call(kernel, out_shape=jax.ShapeDtypeStruct((512, 512), BF16),...  103 us
    unnamed x13, local copies, waits for them, and re-layouts  5.85 us

profile of v3, /device:TPU:1, one launch (start us, length us, event | category | flops | bytes accessed | tf_op | source)
XLA Modules:
  0.0 109.1 jit_solution(17260089685611815003)
XLA Ops:
  0.0 0.7 broadcast_in_dim.8.skip_ref
  0.7 0.0 copy-start
  0.7 1.4 %copy-done = bf16[3,32,8192]{2,1,0:T(8,128)(2,1)S(1)} copy-done((bf16[3,32,8192]{2,1,0:T(8,128)(2,1)S(1)}, bf16[3,32,8192]{2,1,0:T(8,128)(2,1)}, u32[]{:S(2)}) %copy-start) | copy-done | bytes 1572888
  2.1 0.0 copy-start.1
  2.1 0.8 copy-done.1
  2.9 0.0 copy-start.2
  2.9 0.8 copy-done.2
  3.6 0.0 copy-start.3
  3.7 0.8 copy-done.3
  4.4 0.0 copy-start.4
  4.4 0.7 copy-done.4
  5.1 0.0 copy-start.5
  5.1 0.7 copy-done.5
  5.7 102.5 %shard_map.73 = bf16[512,512]{1,0:T(8,128)(2,1)S(1)} custom-call(bf16[3,32,8192]{2,1,0:T(8,128)(2,1)S(1)} %copy-done, s32[1,32]{1,0:T(1,128)S(1)} %copy-done.5, s32[512]{0:T(512)S(1)} %copy-done.4, f32[3,7,512]{2,1,0:T(8,128)S(1)} %copy-done.1, f32[16,512]{1,0:T(8,128)S(1)} %copy-done.2, f32[16,512]{1,0:T(8,128)S(1)} %copy-done.3, ...), custom_call_target="tpu_custom_call" | custom-call | flops 67108864 | bytes 4194304 | tf_op jit(solution)/shard_map/pallas_call | solution.py:349
  108.3 0.8 copy.9
Async XLA Ops:
  0.7 1.4 %copy-start = (bf16[3,32,8192]{2,1,0:T(8,128)(2,1)S(1)}, bf16[3,32,8192]{2,1,0:T(8,128)(2,1)}, u32[]{:S(2)}) copy-start(bf16[3,32,8192]{2,1,0:T(8,128)(2,1)} %a_ref.1) | copy-start | bytes 4718596
  2.1 0.8 copy-start.1
  2.9 0.8 copy-start.2
  3.6 0.8 copy-start.3
  4.4 0.7 copy-start.4
  5.1 0.7 copy-start.5

commit v4 on v3

--- a/solution.py
+++ b/solution.py
@@ -88,6 +88,25 @@
             @pl.when(to != q)
             def _():
                 remote(rows, buf[p].at[q], (to, c), zs.at[p], zr.at[p]).start()
+
+    def forward_far_first(p, first, stop):
+        f, half = PIECES[p]
+
+        @pl.loop(first, stop)
+        def _(i):
+            reach = 8 - (i + 1) // 2
+            target = lax.rem(z + 16 + reach * (2 * lax.rem(i, 2) - 1), 16)
+            shift = lax.rem(target + 16 - c, 16)
+            j = lax.rem(shift + 29 - z, 15) + 1
+
+            @pl.when(shift == 0)
+            def _():
+                ring_send(p, a_ref.at[f, :, columns(c, half)], target)
+
+            @pl.when(shift != 0)
+            def _():
+                remote(mid[p].at[j - 1], mid[p].at[j - 1], (q, c), p1s.at[p], p1r.at[p, j - 1]).wait_recv()
+                ring_send(p, mid[p].at[j - 1], target)
 
     def forward(p, first=0, stop=16):
         f, half = PIECES[p]
@@ -254,7 +273,7 @@
     for o in range(1, 4):
         to = 2 * (4 * group + lax.rem(member + o, 4)) + core
         remote(l1buf.at[member], l1buf.at[member], (to, c), l1s, l1r).start()
-    forward(5, 0, 10)
+    forward_far_first(5, 0, 10)
     remote(l1buf.at[pl.ds(0, 3)], l1buf.at[pl.ds(0, 3)], (q, c), l1s, l1r).wait()
 
     def combine(table, mine, l, count):
@@ -284,7 +303,7 @@
     for o in range(1, 4):
         to = 2 * (4 * lax.rem(group + o, 4) + member) + core
         remote(l2buf.at[group], l2buf.at[group], (to, c), l2s, l2r).start()
-    forward(5, 10, 16)
+    forward_far_first(5, 10, 16)
     remote(l2buf.at[pl.ds(0, 3)], l2buf.at[pl.ds(0, 3)], (q, c), l2s, l2r).wait()
 
     for l in range(4):

time: 111 us -> 112 us (level); the launches traced: 109 us -> 111 us
  Pallas kernels: 103 us -> 105 us
    pallas_call x1, Pallas kernels: 103 us -> 105 us  [on_device(): pl.pallas_call(kernel, out_shape=jax.ShapeDtypeStruct((512, 512), BF16),...]
where the time goes in v4:
time: 112 us; the launch traced here: 111 us
  Pallas kernels  105 us (94%)
  local copies, waits for them, and re-layouts  6.53 us (6%)
    pallas_call x1, Pallas kernels, on_device(): pl.pallas_call(kernel, out_shape=jax.ShapeDtypeStruct((512, 512), BF16),...  105 us
    unnamed x13, local copies, waits for them, and re-layouts  5.85 us

profile of v4, /device:TPU:1, one launch (start us, length us, event | category | flops | bytes accessed | tf_op | source)
XLA Modules:
  0.0 111.3 jit_solution(3418366811615714785)
XLA Ops:
  0.0 0.7 broadcast_in_dim.8.skip_ref
  0.7 0.0 copy-start
  0.7 1.4 %copy-done = bf16[3,32,8192]{2,1,0:T(8,128)(2,1)S(1)} copy-done((bf16[3,32,8192]{2,1,0:T(8,128)(2,1)S(1)}, bf16[3,32,8192]{2,1,0:T(8,128)(2,1)}, u32[]{:S(2)}) %copy-start) | copy-done | bytes 1572888
  2.1 0.0 copy-start.1
  2.1 0.8 copy-done.1
  2.9 0.0 copy-start.2
  2.9 0.8 copy-done.2
  3.6 0.0 copy-start.3
  3.7 0.8 copy-done.3
  4.4 0.0 copy-start.4
  4.4 0.7 copy-done.4
  5.1 0.0 copy-start.5
  5.1 0.7 copy-done.5
  5.7 104.8 %shard_map.73 = bf16[512,512]{1,0:T(8,128)(2,1)S(1)} custom-call(bf16[3,32,8192]{2,1,0:T(8,128)(2,1)S(1)} %copy-done, s32[1,32]{1,0:T(1,128)S(1)} %copy-done.5, s32[512]{0:T(512)S(1)} %copy-done.4, f32[3,7,512]{2,1,0:T(8,128)S(1)} %copy-done.1, f32[16,512]{1,0:T(8,128)S(1)} %copy-done.2, f32[16,512]{1,0:T(8,128)S(1)} %copy-done.3, ...), custom_call_target="tpu_custom_call" | custom-call | flops 67108864 | bytes 4194304 | tf_op jit(solution)/shard_map/pallas_call | solution.py:368
  110.5 0.8 copy.9
Async XLA Ops:
  0.7 1.4 %copy-start = (bf16[3,32,8192]{2,1,0:T(8,128)(2,1)S(1)}, bf16[3,32,8192]{2,1,0:T(8,128)(2,1)}, u32[]{:S(2)}) copy-start(bf16[3,32,8192]{2,1,0:T(8,128)(2,1)} %a_ref.1) | copy-start | bytes 4718596
  2.1 0.8 copy-start.1
  2.9 0.8 copy-start.2
  3.6 0.8 copy-start.3
  4.4 0.7 copy-start.4
  5.1 0.7 copy-start.5
